TPU v7x, 32 devices: a whole 2x2x4 slice. The times are simulated.
32 devices in a mesh: section: 16 (over z, x, core), tensor: 2 (over y).
Axes of the slice: x: 2, y: 2, z: 4, core: 2. Of those that a mesh axis runs over, the one named last changes fastest.
Arguments:
- activations: bfloat16 [16, 256, 4096], P('section', 'tensor'), may hold values from -6 to 6
- upstream_grad: bfloat16 [16, 256, 4096], P('section', 'tensor'), may hold values from -6 to 6
- stash_blocks: bfloat16 [16, 256, 4096], P('section', 'tensor'), may hold values from -6 to 6
- guest_blocks: bfloat16 [16, 256, 4096], P('section', 'tensor'), may hold values from -6 to 6
- norm_gain: float32 [16, 4096], P('section'), may hold values from 0.1 to 1.9
- query_weight: bfloat16 [16, 4096, 4096], P('section', None, 'tensor'), may hold values from -2 to 2
- keyval_weight: bfloat16 [16, 4096, 2, 1024], P('section', None, None, 'tensor'), may hold values from -1 to 1
- output_weight: bfloat16 [16, 4096, 4096], P('section', 'tensor'), may hold values from -0.09375 to 0.09375
- evict_marks: int32 [16, 16], replicated, may hold values from 0 to 1, as said below
Outputs:
- next_input: bfloat16 [16, 256, 4096], P('section', 'tensor')
- prev_grad: bfloat16 [16, 256, 4096], P('section', 'tensor')
- kept_stash: bfloat16 [16, 256, 4096], P('section', 'tensor')
- held_blocks: bfloat16 [16, 256, 4096], P('section', 'tensor')
Inputs may be any that keep to these rules, and one draw needn't show every extreme that they name: `evict_marks`: row s marks with 1 the blocks that section s evicts to section 15 - s; a row has at most 8 ones, row 0 exactly 8, rows of the first half of the sections at least 4.
All inputs are finite; a program needn't handle non-finite values.
Results may differ from a plain program's by a relative error of at most 0.012.
Values may be sent and summed in bfloat16 or wider, within the bound.
No kernel may reach another device: no remote copies, remote signals or barrier semaphores. Data moves between devices by JAX's collectives and lax.ppermute only.
A program may use at most 128 MiB of HBM per device.

v0:
```python
import jax
import jax.numpy as jnp
from jax import lax
from jax.sharding import PartitionSpec as P

HEADS = 32
KV_HEADS = 8
HEAD_DIM = 128


EPSILON = 1e-05
NEG_LARGE = -1e30


def from_partner(x, axis, bit):
    return lax.ppermute(x, axis, [(i, i ^ 1 << bit) for i in range(lax.axis_size(axis))])


def shifted(x, axis, by):
    peers = lax.axis_size(axis)
    pairs = [(i, i + by) for i in range(peers) if 0 <= i + by < peers]
    return lax.ppermute(x, axis, pairs)


def root_norm(features, gain_row):
    values = features.astype(jnp.float32)
    factor = lax.rsqrt(jnp.mean(values * values, axis=-1, keepdims=True) + EPSILON)
    return values * factor * gain_row


def causal_probs(scores):
    length = scores.shape[-1]
    allowed = jnp.arange(length)[:, None] >= jnp.arange(length)[None, :]
    masked = jnp.where(allowed, scores, NEG_LARGE)
    row_max = jnp.max(masked, axis=-1, keepdims=True)
    raised = jnp.exp(masked - row_max)
    return raised / jnp.sum(raised, axis=-1, keepdims=True)


def local(
    activations,
    upstream_grad,
    stash_blocks,
    guest_blocks,
    norm_gain,
    query_weight,
    keyval_weight,
    output_weight,
    evict_marks,
):
    sections = lax.axis_size("section")
    section_index = lax.axis_index("section")
    current = activations[0]
    upstream = upstream_grad[0]
    stash_rows = stash_blocks[0]
    guest_rows = guest_blocks[0]
    row_count, model_width = current.shape
    block_count = evict_marks.shape[1]
    block_rows = row_count // block_count
    own_marks = lax.dynamic_index_in_dim(evict_marks, section_index, 0, keepdims=False)
    own_mask = (jnp.repeat(own_marks, block_rows) == 1)[:, None]
    leaving = jnp.where(own_mask, current, jnp.zeros_like(current))
    payload = jnp.stack([guest_rows, leaving])
    bit_total = sections.bit_length() - 1
    bit_order = list(range(bit_total))
    for bit_number in bit_order:
        payload = from_partner(payload, "section", bit_number)
    returned = payload[0]
    arrived = payload[1]
    back_rows = jnp.where(own_mask, returned, stash_rows)
    kept_rows = jnp.where(own_mask, jnp.zeros_like(current), current)
    gain_row = norm_gain[0]
    query_local = query_weight[0]
    keyval_local = keyval_weight[0]
    output_local = output_weight[0]
    query_width = query_local.shape[1]
    keyval_width = keyval_local.shape[2]
    local_kv_heads = keyval_width // HEAD_DIM
    group_size = HEADS // KV_HEADS
    head_scale = HEAD_DIM ** (-0.5)
    keyval_flat = keyval_local.reshape(model_width, 2 * keyval_width)
    normed_now = root_norm(current, gain_row).astype(jnp.bfloat16)
    normed_back = root_norm(back_rows, gain_row).astype(jnp.bfloat16)
    stacked = jnp.stack([normed_now, normed_back, upstream], axis=1)
    fragment = lax.all_gather(stacked, "tensor", axis=0, tiled=True)
    outputs = [
        jnp.dot(fragment[:, 0], query_local, preferred_element_type=jnp.float32),
        jnp.dot(fragment[:, 0], keyval_flat, preferred_element_type=jnp.float32),
        jnp.dot(fragment[:, 1], query_local, preferred_element_type=jnp.float32),
        jnp.dot(fragment[:, 1], keyval_flat, preferred_element_type=jnp.float32),
        jnp.einsum("rd,cd->rc", fragment[:, 2], output_local, preferred_element_type=jnp.float32),
    ]
    projected = jnp.concatenate([result.astype(jnp.bfloat16) for result in outputs], axis=1)
    length = projected.shape[0]
    edge_two = query_width + 2 * keyval_width
    edge_three = edge_two + query_width
    edge_four = edge_three + 2 * keyval_width
    query_now = projected[:, :query_width].reshape(length, local_kv_heads, group_size, HEAD_DIM)
    keyval_now = projected[:, query_width:edge_two].reshape(length, 2, local_kv_heads, HEAD_DIM)
    query_back = projected[:, edge_two:edge_three].reshape(
        length, local_kv_heads, group_size, HEAD_DIM
    )
    keyval_back = projected[:, edge_three:edge_four].reshape(length, 2, local_kv_heads, HEAD_DIM)
    grad_context = projected[:, edge_four:].reshape(length, local_kv_heads, group_size, HEAD_DIM)
    scores_now = jnp.einsum(
        "tkgh,ukh->kgtu", query_now, keyval_now[:, 0], preferred_element_type=jnp.float32
    )
    probs_now = causal_probs(scores_now * head_scale)
    weights_now = probs_now.astype(jnp.bfloat16)
    context_now = jnp.einsum(
        "kgtu,ukh->tkgh", weights_now, keyval_now[:, 1], preferred_element_type=jnp.float32
    )
    context_flat = context_now.astype(jnp.bfloat16).reshape(length, query_width)
    key_back = keyval_back[:, 0]
    value_back = keyval_back[:, 1]
    scores_back = jnp.einsum(
        "tkgh,ukh->kgtu", query_back, key_back, preferred_element_type=jnp.float32
    )
    probs_back = causal_probs(scores_back * head_scale)
    weights_back = probs_back.astype(jnp.bfloat16)
    grad_value = jnp.einsum(
        "kgtu,tkgh->ukh", weights_back, grad_context, preferred_element_type=jnp.float32
    ).astype(jnp.bfloat16)
    grad_prob = jnp.einsum(
        "tkgh,ukh->kgtu", grad_context, value_back, preferred_element_type=jnp.float32
    )
    grad_score = (
        probs_back
        * (grad_prob - jnp.sum(probs_back * grad_prob, axis=-1, keepdims=True))
        * head_scale
    )
    grad_score = grad_score.astype(jnp.bfloat16)
    grad_query = jnp.einsum(
        "kgtu,ukh->tkgh", grad_score, key_back, preferred_element_type=jnp.float32
    )
    grad_query = grad_query.astype(jnp.bfloat16).reshape(length, query_width)
    grad_key = jnp.einsum(
        "kgtu,tkgh->ukh", grad_score, query_back, preferred_element_type=jnp.float32
    ).astype(jnp.bfloat16)
    grad_keyval = jnp.stack([grad_key, grad_value], axis=1).reshape(length, 2, keyval_width)
    forward_term = jnp.dot(context_flat, output_local, preferred_element_type=jnp.float32)
    backward_term = jnp.einsum(
        "tc,dc->td", grad_query, query_local, preferred_element_type=jnp.float32
    )
    backward_term = backward_term + jnp.einsum(
        "tjc,djc->td", grad_keyval, keyval_local, preferred_element_type=jnp.float32
    )
    rounded = lax.optimization_barrier(
        jnp.stack([forward_term, backward_term], axis=1).astype(jnp.bfloat16)
    )
    summed = lax.psum(rounded.astype(jnp.float32).astype(jnp.bfloat16), "tensor").astype(
        jnp.float32
    )
    own_share = lax.dynamic_slice_in_dim(summed, lax.axis_index("tensor") * row_count, row_count, 0)
    updated = (current.astype(jnp.float32) + own_share[:, 0]).astype(jnp.bfloat16)
    normed_out, pull_back = jax.vjp(
        lambda inputs: root_norm(inputs, gain_row), back_rows.astype(jnp.float32)
    )
    norm_grad = pull_back(own_share[:, 1])[0]
    passed = (upstream.astype(jnp.float32) + norm_grad).astype(jnp.bfloat16)
    sent_forward = shifted(updated[None], "section", 1)
    sent_back = shifted(passed[None], "section", -1)
    return (sent_forward, sent_back, kept_rows[None], arrived[None])


def solution(mesh):
    placed = (
        P("section", "tensor", None),
        P("section", "tensor", None),
        P("section", "tensor", None),
        P("section", "tensor", None),
        P("section", None),
        P("section", None, "tensor"),
        P("section", None, None, "tensor"),
        P("section", "tensor", None),
        P(),
    )
    return jax.shard_map(
        local,
        mesh=mesh,
        in_specs=placed,
        out_specs=(
            P("section", "tensor", None),
            P("section", "tensor", None),
            P("section", "tensor", None),
            P("section", "tensor", None),
        ),
        check_vma=False,
    )
```

profile of v0, /device:TPU:1, one launch (start us, length us, event | category | flops | bytes accessed | tf_op | source)
XLA Modules:
  0.0 563.1 jit_solution(5850173914765885181)
XLA Ops:
  8.2 2.5 broadcast_select_fusion
  12.3 4.1 collective-permute-done
  16.4 2.3 collective-permute-start.1
  18.7 45.7 %collective-permute-done.1 = bf16[2,128,4096]{2,1,0:T(8,128)(2,1)S(1)} collective-permute-done((bf16[2,128,4096]{2,1,0:T(8,128)(2,1)S(1)}, bf16[2,128,4096]{2,1,0:T(8,128)(2,1)S(1)}, u32[]{:S(2)}, u32[]{:S(2)}) %collective-permute-start.1) | collective-permute-done | bytes 2097184 | tf_op jit(solution)/shard_map/ppermute | solution.py:16
  65.6 45.0 %collective-permute-done.2 = bf16[2,128,4096]{2,1,0:T(8,128)(2,1)S(1)} collective-permute-done((bf16[2,128,4096]{2,1,0:T(8,128)(2,1)S(1)}, bf16[2,128,4096]{2,1,0:T(8,128)(2,1)S(1)}, u32[]{:S(2)}, u32[]{:S(2)}) %collective-permute-start.2) | collective-permute-done | bytes 2097184 | tf_op jit(solution)/shard_map/ppermute | solution.py:16
  112.9 90.5 %collective-permute-done.3 = bf16[2,128,4096]{2,1,0:T(8,128)(2,1)S(1)} collective-permute-done((bf16[2,128,4096]{2,1,0:T(8,128)(2,1)S(1)}, bf16[2,128,4096]{2,1,0:T(8,128)(2,1)S(1)}, u32[]{:S(2)}, u32[]{:S(2)}) %collective-permute-start.3) | collective-permute-done | bytes 2097184 | tf_op jit(solution)/shard_map/ppermute | solution.py:16
  205.7 2.0 pad_maximum_fusion.1
  207.9 10.1 %copy.66 = bf16[512,8,2,512]{3,1,2,0:T(8,128)(2,1)} copy(bf16[512,8,2,512]{3,2,1,0:T(2,128)(2,1)} %bitcast.224) | data formatting | bytes 16777216
  218.0 71.4 %all-gather.2.cloned.1.call-done = bf16[256,3,4096]{2,0,1:T(8,128)(2,1)} async-done(((bf16[128,3,4096]{2,0,1:T(8,128)(2,1)}), bf16[256,3,4096]{2,0,1:T(8,128)(2,1)}) %all-gather.2.cloned.1.call-update) | async-done | bytes 6291472 | tf_op jit(solution)/shard_map/all_gather | solution.py:85
  289.4 10.9 %fusion.41 = bf16[256,2048]{1,0:T(8,128)(2,1)S(1)} fusion(bf16[1,4096,2048]{2,1,0:T(8,128)(2,1)} %param.14, bf16[256,3,4096]{2,0,1:T(8,128)(2,1)} %all-gather.2.cloned.1.call-done), kind=kOutput, calls=%fused_computation.42 | convolution fusion | flops 4295491584 | bytes 19922944 | tf_op jit(solution)/shard_map/dot_general | solution.py:89
  301.6 11.9 %fusion.44 = bf16[256,2048]{1,0:T(8,128)(2,1)} fusion(bf16[1,2048,4096]{2,1,0:T(8,128)(2,1)} %param.16, bf16[256,3,4096]{2,0,1:T(8,128)(2,1)} %all-gather.2.cloned.1.call-done), kind=kOutput, calls=%fused_computation.43 | convolution fusion | flops 4295491584 | bytes 19922944 | tf_op jit(solution)/shard_map/rd,cd->rc/dot_general | solution.py:91
  315.4 7.1 %fusion.73 = bf16[256,1024]{1,0:T(8,128)(2,1)} fusion(bf16[4096,1024]{1,0:T(8,128)(2,1)} %bitcast.226, bf16[256,3,4096]{2,0,1:T(8,128)(2,1)} %all-gather.2.cloned.1.call-done), kind=kOutput, calls=%fused_computation.80 | convolution fusion | flops 2147745792 | bytes 11010048 | tf_op jit(solution)/shard_map/dot_general | solution.py:90
  322.6 2.2 reshape.312
  326.0 2.7 fusion.90
  328.6 4.8 fusion.105
  333.4 3.8 fusion.79
  337.2 8.2 %fusion.82 = bf16[4,128,256]{2,1,0:T(8,128)(2,1)} fusion(bf16[256,4,4,128]{0,3,2,1:T(8,128)(2,1)} %bitcast.233, f32[4,256,256,4]{2,1,3,0:T(8,128)} %fusion.90, f32[4,4,256,256]{2,3,1,0:T(8,128)} %get-tuple-element.15, f32[4,4,256]{2,1,0:T(4,128)S(1)} %get-tuple-element.14), kind=kOutput, calls=%fused_computation.85 | convolution fusion | flops 275910912 | bytes 9715712 | tf_op jit(solution)/shard_map/kgtu,tkgh->ukh/dot_general | solution.py:137
  345.4 8.2 %fusion.72 = bf16[4,128,4,256]{3,1,2,0:T(8,128)(2,1)} fusion(f32[4,256,256,4]{2,1,3,0:T(8,128)} %fusion.90, bf16[256,1,4,128]{3,2,1,0:T(4,128)(2,1)S(1)} %get-tuple-element.10, f32[4,4,256,256]{2,3,1,0:T(8,128)} %get-tuple-element.15, f32[4,4,256]{2,1,0:T(4,128)S(1)} %get-tuple-element.14), kind=kOutput, calls=%fused_computation.79 | convolution fusion | flops 276304128 | bytes 9715712 | tf_op jit(solution)/shard_map/kgtu,ukh->tkgh/dot_general | solution.py:133
  353.7 11.9 %fusion.38 = bf16[256,2048]{1,0:T(8,128)(2,1)} fusion(bf16[1,4096,2048]{2,1,0:T(8,128)(2,1)} %param.14, bf16[256,3,4096]{2,0,1:T(8,128)(2,1)} %all-gather.2.cloned.1.call-done), kind=kOutput, calls=%fused_computation.41 | convolution fusion | flops 4295491584 | bytes 19922944 | tf_op jit(solution)/shard_map/dot_general | solution.py:87
  365.5 2.0 reshape.310
  367.5 7.1 %fusion.74 = bf16[256,1024]{1,0:T(8,128)(2,1)} fusion(bf16[4096,1024]{1,0:T(8,128)(2,1)} %bitcast.227, bf16[256,3,4096]{2,0,1:T(8,128)(2,1)} %all-gather.2.cloned.1.call-done), kind=kOutput, calls=%fused_computation.81 | convolution fusion | flops 2147745792 | bytes 11010048 | tf_op jit(solution)/shard_map/dot_general | solution.py:88
  374.6 2.2 reshape.309
  386.3 5.7 %fusion.27 = bf16[256,1,4096]{2,0,1:T(8,128)(2,1)} fusion(bf16[256,2048]{0,1:T(8,128)(2,1)S(1)} %bitcast.231, bf16[1,2048,4096]{2,1,0:T(8,128)(2,1)S(1)} %bitcast.223), kind=kOutput, calls=%fused_computation.19 | convolution fusion | flops 4296015872 | bytes 19922944 | tf_op jit(solution)/shard_map/dot_general | solution.py:141
  392.4 12.6 %fusion.7 = f32[256,4096]{1,0:T(8,128)} fusion(bf16[256,2048]{0,1:T(8,128)(2,1)} %bitcast.239, bf16[1,4096,2048]{2,1,0:T(8,128)(2,1)} %param.14), kind=kOutput, calls=%fused_computation.7 | convolution fusion | flops 4294967296 | bytes 22020096 | tf_op jit(solution)/shard_map/tc,dc->td/dot_general | solution.py:142
  405.0 7.1 %fusion.30 = bf16[256,1,4096]{2,0,1:T(8,128)(2,1)S(1)} fusion(f32[256,4096]{1,0:T(8,128)} %fusion.7, bf16[4096,2,512]{2,1,0:T(2,128)(2,1)} %bitcast.225, bf16[256,1,512]{2,0,1:T(8,128)(2,1)S(1)} %copy.45, bf16[256,1,512]{2,0,1:T(8,128)(2,1)S(1)} %copy.44), kind=kOutput, calls=%fused_computation.20 | convolution fusion | flops 2149842944 | bytes 15204352 | tf_op jit(solution)/shard_map/tjc,djc->td/dot_general | solution.py:145
  412.1 2.3 pad_maximum_fusion
  414.5 108.0 %all-reduce.2.cloned.1.call-done = bf16[256,2,4096]{2,0,1:T(8,128)(2,1)} async-done(((bf16[256,2,4096]{2,0,1:T(8,128)(2,1)}), bf16[256,2,4096]{2,0,1:T(8,128)(2,1)}) %all-reduce.2.cloned.1.call-update) | async-done | bytes 4194320 | tf_op jit(solution)/shard_map/psum | solution.py:151
  522.5 2.2 dynamic-slice_convert_fusion
  526.6 2.6 collective-permute-start.5
  529.2 3.0 collective-permute-start.4
  533.3 9.5 %collective-permute-done.5 = bf16[1,128,4096]{2,1,0:T(8,128)(2,1)S(1)} collective-permute-done((bf16[1,128,4096]{2,1,0:T(8,128)(2,1)S(1)}, bf16[1,128,4096]{2,1,0:T(8,128)(2,1)S(1)}, u32[]{:S(2)}, u32[]{:S(2)}) %collective-permute-start.5) | collective-permute-done | bytes 1048608 | tf_op jit(solution)/shard_map/ppermute | solution.py:22
  542.8 11.4 %collective-permute-done.4 = bf16[1,128,4096]{2,1,0:T(8,128)(2,1)S(1)} collective-permute-done((bf16[1,128,4096]{2,1,0:T(8,128)(2,1)S(1)}, bf16[1,128,4096]{2,1,0:T(8,128)(2,1)S(1)}, u32[]{:S(2)}, u32[]{:S(2)}) %collective-permute-start.4) | collective-permute-done | bytes 1048608 | tf_op jit(solution)/shard_map/ppermute | solution.py:22
  (64 shorter events, 27.6 us)
Async XLA Ops:
  7.2 105.4 %copy-start = (bf16[1,128,4096]{2,1,0:T(8,128)(2,1)S(1)}, bf16[1,128,4096]{2,1,0:T(8,128)(2,1)}, u32[]{:S(2)}) copy-start(bf16[1,128,4096]{2,1,0:T(8,128)(2,1)} %param.9) | copy-start | bytes 3145732
  7.2 282.2 %all-gather.2.cloned.1.call-start = ((), (), s32[]{:S(2)}) async-start(), calls=%async_computation | async-start | bytes 9437184 | tf_op jit(solution)/shard_map/all_gather | solution.py:85
  8.2 195.2 %copy-start.1 = (bf16[1,128,4096]{2,1,0:T(8,128)(2,1)S(1)}, bf16[1,128,4096]{2,1,0:T(8,128)(2,1)}, u32[]{:S(2)}) copy-start(bf16[1,128,4096]{2,1,0:T(8,128)(2,1)} %param.11) | copy-start | bytes 3145732
  10.7 194.1 %copy-start.10 = (f32[1,4096]{1,0:T(1,128)S(1)}, f32[1,4096]{1,0:T(1,128)}, u32[]{:S(2)}) copy-start(f32[1,4096]{1,0:T(1,128)} %param.13) | copy-start | bytes 49156
  12.1 193.5 %copy-start.5 = (bf16[1,128,4096]{2,1,0:T(8,128)(2,1)S(1)}, bf16[1,128,4096]{2,1,0:T(8,128)(2,1)}, u32[]{:S(2)}) copy-start(bf16[1,128,4096]{2,1,0:T(8,128)(2,1)} %param.10) | copy-start | bytes 3145732
  12.1 4.2 collective-permute-start
  16.4 48.0 %collective-permute-start.1 = (bf16[2,128,4096]{2,1,0:T(8,128)(2,1)S(1)}, bf16[2,128,4096]{2,1,0:T(8,128)(2,1)S(1)}, u32[]{:S(2)}, u32[]{:S(2)}) collective-permute-start(bf16[2,128,4096]{2,1,0:T(8,128)(2,1)S(1)} %collective-permute-done), channel_id=1, source_target_pairs={{0,4},{2,6},{4,0},{6,2},{8,12},{10,14},{12,8},{14,10},{16,20},{18,... | collective-permute-start | bytes 6291464 | tf_op jit(solution)/shard_map/ppermute | solution.py:16
  64.4 46.3 %collective-permute-start.2 = (bf16[2,128,4096]{2,1,0:T(8,128)(2,1)S(1)}, bf16[2,128,4096]{2,1,0:T(8,128)(2,1)S(1)}, u32[]{:S(2)}, u32[]{:S(2)}) collective-permute-start(bf16[2,128,4096]{2,1,0:T(8,128)(2,1)S(1)} %collective-permute-done.1), channel_id=1, source_target_pairs={{0,8},{2,10},{4,12},{6,14},{8,0},{10,2},{12,4},{14,6},{16,24},{18,... | collective-permute-start | bytes 6291464 | tf_op jit(solution)/shard_map/ppermute | solution.py:16
  110.7 92.7 %collective-permute-start.3 = (bf16[2,128,4096]{2,1,0:T(8,128)(2,1)S(1)}, bf16[2,128,4096]{2,1,0:T(8,128)(2,1)S(1)}, u32[]{:S(2)}, u32[]{:S(2)}) collective-permute-start(bf16[2,128,4096]{2,1,0:T(8,128)(2,1)S(1)} %collective-permute-done.2), channel_id=1, source_target_pairs={{0,16},{2,18},{4,20},{6,22},{8,24},{10,26},{12,28},{14,30},{16,0},... | collective-permute-start | bytes 6291464 | tf_op jit(solution)/shard_map/ppermute | solution.py:16
  203.4 1.4 copy-start.2
  207.7 314.8 %all-reduce.2.cloned.1.call-start = ((), (), s32[]{:S(2)}) async-start(), calls=%async_computation.1 | async-start | bytes 8388608 | tf_op jit(solution)/shard_map/psum | solution.py:151
  379.6 3.6 slice-start
  381.4 1.3 copy-start.9
  381.4 2.4 slice-start.1
  381.5 3.5 slice-start.2
  382.7 3.6 slice-start.3
  386.3 5.7 %copy-start.8 = (bf16[4,128,256]{2,1,0:T(8,128)(2,1)S(1)}, bf16[4,128,256]{2,1,0:T(8,128)(2,1)}, u32[]{:S(2)}) copy-start(bf16[4,128,256]{2,1,0:T(8,128)(2,1)} %fusion.82) | copy-start | bytes 786436
  386.3 5.9 %copy-start.7 = (bf16[4,128,256]{2,1,0:T(8,128)(2,1)S(1)}, bf16[4,128,256]{2,1,0:T(8,128)(2,1)}, u32[]{:S(2)}) copy-start(bf16[4,128,256]{2,1,0:T(8,128)(2,1)} %fusion.79) | copy-start | bytes 786436
  405.0 7.1 %copy-start.4 = (bf16[256,1,4096]{2,0,1:T(8,128)(2,1)S(1)}, bf16[256,1,4096]{2,0,1:T(8,128)(2,1)}, u32[]{:S(2)}) copy-start(bf16[256,1,4096]{2,0,1:T(8,128)(2,1)} %fusion.27) | copy-start | bytes 6291460
  414.5 110.9 %copy-start.6 = (bf16[1,128,4096]{2,1,0:T(8,128)(2,1)S(1)}, bf16[1,128,4096]{2,1,0:T(8,128)(2,1)}, u32[]{:S(2)}) copy-start(bf16[1,128,4096]{2,1,0:T(8,128)(2,1)} %param.10) | copy-start | bytes 3145732
  522.5 2.2 copy-start.3
  526.6 16.1 %collective-permute-start.5 = (bf16[1,128,4096]{2,1,0:T(8,128)(2,1)S(1)}, bf16[1,128,4096]{2,1,0:T(8,128)(2,1)S(1)}, u32[]{:S(2)}, u32[]{:S(2)}) collective-permute-start(bf16[1,128,4096]{2,1,0:T(8,128)(2,1)S(1)} %get-tuple-element.4), channel_id=1, source_target_pairs={{2,0},{4,2},{6,4},{8,6},{10,8},{12,10},{14,12},{16,14},{18,16},{20... | collective-permute-start | bytes 3145736 | tf_op jit(solution)/shard_map/ppermute | solution.py:22
  529.2 24.9 %collective-permute-start.4 = (bf16[1,128,4096]{2,1,0:T(8,128)(2,1)S(1)}, bf16[1,128,4096]{2,1,0:T(8,128)(2,1)S(1)}, u32[]{:S(2)}, u32[]{:S(2)}) collective-permute-start(bf16[1,128,4096]{2,1,0:T(8,128)(2,1)S(1)} %get-tuple-element.5), channel_id=1, source_target_pairs={{0,2},{2,4},{4,6},{6,8},{8,10},{10,12},{12,14},{14,16},{16,18},{18... | collective-permute-start | bytes 3145736 | tf_op jit(solution)/shard_map/ppermute | solution.py:22
Sparse Core Ops, SparseCore 0:
  207.8 81.5 all-gather.1
  414.6 107.8 all-reduce.1
where the time goes:
time: 566 us; the launch traced here: 563 us
  waiting for transfers between devices  386 us (68%)
  matrix products  104 us (18%)
  local copies, waits for them, and re-layouts  31.1 us (5%)
  other arithmetic  16.1 us (3%)
  between operations  14.5 us (3%)
  starting transfers between devices  11.4 us (2%)
    ppermute x4, waiting for transfers between devices, from_partner(): lax.ppermute(x, axis, [(i, i ^ 1 << bit) for i in range(lax.axis_size(axi...  185 us
    psum x1, waiting for transfers between devices, local(): lax.psum(rounded.astype(jnp.float32).astype(jnp.bfloat16), 'tensor')  108 us
    all_gather x1, waiting for transfers between devices, local(): fragment = lax.all_gather(stacked, 'tensor', axis=0, tiled=True)  71.4 us
    ppermute x2, waiting for transfers between devices, shifted(): return lax.ppermute(x, axis, pairs)  20.9 us
    unnamed x34, local copies, waits for them, and re-layouts  17 us
    dot_general x1, matrix products, local(): jnp.einsum('tc,dc->td', grad_query, query_local, preferred_element_type=j...  12.6 us
    dot_general x1, matrix products, local(): jnp.einsum('rd,cd->rc', fragment[:, 2], output_local, preferred_element_t...  11.9 us
    dot_general x1, matrix products, local(): jnp.dot(fragment[:, 0], query_local, preferred_element_type=jnp.float32)  11.9 us
  transfers between devices with their start and end apart: 8, of which 8 were waited for; matrix products, arithmetic and copies ran while one was open for 2% of the time, Pallas kernels for 0%

commit v1 on v0

v1 whole, which is shorter than its diff:
```python
import jax
import jax.numpy as jnp
from jax import lax
from jax.experimental import pallas as pl
from jax.experimental.pallas import tpu as pltpu
from jax.sharding import PartitionSpec as P

HEADS = 32
KV_HEADS = 8
HEAD_DIM = 128
GROUP = HEADS // KV_HEADS
MOST_EVICT = 8

EPSILON = 1e-05
NEG_LARGE = -1e30
SCALE = HEAD_DIM ** (-0.5)
ROW_STEP = 16
VMEM_BYTES = 56 * 1024 * 1024


def shifted(x, axis, by):
    peers = lax.axis_size(axis)
    pairs = [(i, i + by) for i in range(peers) if 0 <= i + by < peers]
    return lax.ppermute(x, axis, pairs)


def crossed(x, by):
    peers = lax.axis_size("section")
    pairs = [
        (i * 2 + j, (i + by) * 2 + 1 - j) for i in range(peers) if 0 <= i + by < peers for j in (0, 1)
    ]
    return lax.ppermute(x, ("section", "tensor"), pairs)


def mirrored(x):
    peers = lax.axis_size("section")
    return lax.ppermute(x, "section", [(i, peers - 1 - i) for i in range(peers)])


def swapped(x):
    return lax.ppermute(x, "tensor", [(0, 1), (1, 0)])


def nn(a, b):
    return lax.dot_general(a, b, (((1,), (0,)), ((), ())), preferred_element_type=jnp.float32)


def nt(a, b):
    return lax.dot_general(a, b, (((1,), (1,)), ((), ())), preferred_element_type=jnp.float32)


def tn(a, b):
    return lax.dot_general(a, b, (((0,), (0,)), ((), ())), preferred_element_type=jnp.float32)


def norm_rows(source, target, at, gain):
    @pl.loop(0, source.shape[0] // ROW_STEP)
    def _(step):
        start = pl.multiple_of(step * ROW_STEP, ROW_STEP)
        rows = source[pl.ds(start, ROW_STEP), :].astype(jnp.float32)
        factor = lax.rsqrt(jnp.mean(rows * rows, axis=-1, keepdims=True) + EPSILON)
        target[pl.ds(pl.multiple_of(at + start, ROW_STEP), ROW_STEP), :] = (
            rows * factor * gain
        ).astype(jnp.bfloat16)


def columns_of(left, weight, target, width):
    @pl.loop(0, weight.shape[1] // width)
    def _(step):
        at = pl.ds(pl.multiple_of(step * width, width), width)
        target[:, at] = nn(left[...], weight[:, at]).astype(target.dtype)


def causal_mask(first, length):
    def tokens(dim):
        place = lax.broadcasted_iota(jnp.int32, (length, length), dim) + first
        return jnp.where(place >= length, place - length, place)

    return tokens(0) >= tokens(1)


def causal_probs(queries, keys, allowed):
    scores = jnp.where(allowed, nt(queries, keys) * SCALE, NEG_LARGE)
    raised = jnp.exp(scores - jnp.max(scores, axis=-1, keepdims=True))
    return raised * (1.0 / jnp.sum(raised, axis=-1, keepdims=True))


def head_at(h):
    return slice(h * HEAD_DIM, (h + 1) * HEAD_DIM)


def forward_kernel(
    first_ref, own_ref, rest_ref, gain_ref, wq_ref, wkv_ref, wo_ref,
    own_out, rest_out, normed, total, query, keyval, context,
):
    group = pl.program_id(0)
    row_count = own_ref.shape[0]
    length, width = normed.shape

    @pl.when(group == 0)
    def _():
        norm_rows(own_ref, normed, 0, gain_ref[...])
        norm_rows(rest_ref, normed, row_count, gain_ref[...])

    columns_of(normed, wkv_ref, keyval, 2 * HEAD_DIM)
    columns_of(normed, wq_ref, query, 2 * HEAD_DIM)
    allowed = causal_mask(first_ref[0], length)
    keys, values = keyval[:, :HEAD_DIM], keyval[:, HEAD_DIM:]
    for h in range(GROUP):
        weights = causal_probs(query[:, head_at(h)], keys, allowed).astype(jnp.bfloat16)
        context[:, head_at(h)] = nn(weights, values).astype(jnp.bfloat16)

    step_width = 512

    @pl.loop(0, width // step_width)
    def _(step):
        at = pl.ds(pl.multiple_of(step * step_width, step_width), step_width)
        part = nn(context[...], wo_ref[:, at])

        @pl.when(group == 0)
        def _():
            total[:, at] = part

        @pl.when(group > 0)
        def _():
            total[:, at] += part

    @pl.when(group == pl.num_programs(0) - 1)
    def _():
        own_out[...] = (own_ref[...].astype(jnp.float32) + total[:row_count, :]).astype(jnp.bfloat16)
        rest_out[...] = total[row_count:, :].astype(jnp.bfloat16)


def backward_kernel(
    first_ref, own_ref, rest_ref, up_own_ref, up_rest_ref, gain_ref, wq_ref, wkv_ref, wo_ref,
    own_out, rest_out, normed, upstream, total, query, keyval, grad_context, grad_query, grad_keyval,
):
    group = pl.program_id(0)
    row_count = own_ref.shape[0]
    length, width = normed.shape

    @pl.when(group == 0)
    def _():
        norm_rows(own_ref, normed, 0, gain_ref[...])
        norm_rows(rest_ref, normed, row_count, gain_ref[...])
        upstream[:row_count, :] = up_own_ref[...]
        upstream[row_count:, :] = up_rest_ref[...]

    columns_of(normed, wkv_ref, keyval, 2 * HEAD_DIM)
    columns_of(normed, wq_ref, query, 2 * HEAD_DIM)

    @pl.loop(0, wo_ref.shape[0] // (2 * HEAD_DIM))
    def _(step):
        at = pl.ds(pl.multiple_of(step * 2 * HEAD_DIM, 2 * HEAD_DIM), 2 * HEAD_DIM)
        grad_context[:, at] = nt(upstream[...], wo_ref[at, :]).astype(jnp.bfloat16)

    allowed = causal_mask(first_ref[0], length)
    keys, values = keyval[:, :HEAD_DIM], keyval[:, HEAD_DIM:]
    grad_key = grad_value = None
    for h in range(GROUP):
        queries, grads = query[:, head_at(h)], grad_context[:, head_at(h)]
        probs = causal_probs(queries, keys, allowed)
        value_part = tn(probs.astype(jnp.bfloat16), grads)
        grad_prob = nt(grads, values)
        mean_grad = jnp.sum(probs * grad_prob, axis=-1, keepdims=True)
        grad_score = (probs * (grad_prob - mean_grad) * SCALE).astype(jnp.bfloat16)
        grad_query[:, head_at(h)] = nn(grad_score, keys).astype(jnp.bfloat16)
        key_part = tn(grad_score, queries)
        grad_key = key_part if h == 0 else grad_key + key_part
        grad_value = value_part if h == 0 else grad_value + value_part
    grad_keyval[:, :HEAD_DIM] = grad_key.astype(jnp.bfloat16)
    grad_keyval[:, HEAD_DIM:] = grad_value.astype(jnp.bfloat16)

    step_width = 512

    @pl.loop(0, width // step_width)
    def _(step):
        at = pl.ds(pl.multiple_of(step * step_width, step_width), step_width)
        part = nt(grad_query[...], wq_ref[at, :]) + nt(grad_keyval[...], wkv_ref[at, :])

        @pl.when(group == 0)
        def _():
            total[:, at] = part

        @pl.when(group > 0)
        def _():
            total[:, at] += part

    @pl.when(group == pl.num_programs(0) - 1)
    def _():
        gain = gain_ref[...]

        def norm_grad(rows, grads):
            factor = lax.rsqrt(jnp.mean(rows * rows, axis=-1, keepdims=True) + EPSILON)
            grads = grads * gain
            mean = jnp.mean(rows * grads, axis=-1, keepdims=True)
            return grads * factor - rows * (factor * factor * factor * mean)

        @pl.loop(0, row_count // ROW_STEP)
        def _(step):
            at = pl.ds(pl.multiple_of(step * ROW_STEP, ROW_STEP), ROW_STEP)
            grads = norm_grad(own_ref[at, :].astype(jnp.float32), total[at, :])
            own_out[at, :] = (up_own_ref[at, :].astype(jnp.float32) + grads).astype(jnp.bfloat16)

        @pl.loop(0, (length - row_count) // ROW_STEP)
        def _(step):
            start = pl.multiple_of(step * ROW_STEP, ROW_STEP)
            at = pl.ds(start, ROW_STEP)
            among = pl.ds(pl.multiple_of(row_count + start, ROW_STEP), ROW_STEP)
            grads = norm_grad(rest_ref[at, :].astype(jnp.float32), total[among, :])
            rest_out[at, :] = grads.astype(jnp.bfloat16)


def layer_call(kernel, first, row_arrays, gain, weights, scratch, flops, name):
    query_weight, keyval_weight, output_weight = weights
    width = query_weight.shape[0]
    groups = keyval_weight.shape[1] // (2 * HEAD_DIM)
    own, rest = row_arrays[:2]
    whole = lambda shape: pl.BlockSpec(shape, lambda g: (0, 0))
    read = sum(x.size for x in (*row_arrays, *weights)) * 2
    return pl.pallas_call(
        kernel,
        grid=(groups,),
        in_specs=[
            pl.BlockSpec(memory_space=pltpu.SMEM),
            *(whole(x.shape) for x in row_arrays),
            whole(gain.shape),
            pl.BlockSpec((width, GROUP * HEAD_DIM), lambda g: (0, g)),
            pl.BlockSpec((width, 2 * HEAD_DIM), lambda g: (0, g)),
            pl.BlockSpec((GROUP * HEAD_DIM, width), lambda g: (g, 0)),
        ],
        out_specs=[whole(own.shape), whole(rest.shape)],
        out_shape=[
            jax.ShapeDtypeStruct(own.shape, jnp.bfloat16),
            jax.ShapeDtypeStruct(rest.shape, jnp.bfloat16),
        ],
        scratch_shapes=scratch,
        compiler_params=pltpu.CompilerParams(vmem_limit_bytes=VMEM_BYTES),
        cost_estimate=pl.CostEstimate(flops=flops, bytes_accessed=read, transcendentals=0),
        name=name,
    )(first, *row_arrays, gain, *weights)


def forward_layer(first, own, rest, gain, weights):
    length, width = own.shape[0] + rest.shape[0], own.shape[1]
    cols = GROUP * HEAD_DIM
    scratch = [
        pltpu.VMEM((length, width), jnp.bfloat16),
        pltpu.VMEM((length, width), jnp.float32),
        pltpu.VMEM((length, cols), jnp.bfloat16),
        pltpu.VMEM((length, 2 * HEAD_DIM), jnp.bfloat16),
        pltpu.VMEM((length, cols), jnp.bfloat16),
    ]
    flops = 2 * length * sum(x.size for x in weights)
    return layer_call(forward_kernel, first, (own, rest), gain, weights, scratch, flops, "forward_layer")


def backward_layer(first, own, rest, up_own, up_rest, gain, weights):
    length, width = own.shape[0] + rest.shape[0], own.shape[1]
    cols = GROUP * HEAD_DIM
    scratch = [
        pltpu.VMEM((length, width), jnp.bfloat16),
        pltpu.VMEM((length, width), jnp.bfloat16),
        pltpu.VMEM((length, width), jnp.float32),
        pltpu.VMEM((length, cols), jnp.bfloat16),
        pltpu.VMEM((length, 2 * HEAD_DIM), jnp.bfloat16),
        pltpu.VMEM((length, cols), jnp.bfloat16),
        pltpu.VMEM((length, cols), jnp.bfloat16),
        pltpu.VMEM((length, 2 * HEAD_DIM), jnp.bfloat16),
    ]
    flops = 2 * length * (sum(x.size for x in weights) + weights[0].size + weights[1].size)
    rows = (own, rest, up_own, up_rest)
    return layer_call(backward_kernel, first, rows, gain, weights, scratch, flops, "backward_layer")


def packing(marks, row_count):
    block_rows = row_count // marks.shape[0]
    rank = jnp.cumsum(marks) - 1
    place = jnp.repeat(rank, block_rows) * block_rows + jnp.arange(row_count) % block_rows
    chosen = jnp.repeat(marks, block_rows) == 1
    place = jnp.where(chosen, place, -1)
    slots = jnp.arange(MOST_EVICT * block_rows)
    return (place[None, :] == slots[:, None]).astype(jnp.bfloat16), chosen[:, None]


def others_rows(x):
    if lax.axis_size("tensor") == 2:
        return swapped(x)
    row_count = x.shape[0]
    rows = lax.all_gather(x, "tensor", axis=0, tiled=True)
    return jnp.roll(rows, -row_count * lax.axis_index("tensor"), axis=0)[row_count:]


def summed_and_moved(own, rest, by):
    if lax.axis_size("tensor") == 2:
        base, term = shifted(own, "section", by), crossed(rest, by)
        return (base.astype(jnp.float32) + term.astype(jnp.float32)).astype(jnp.bfloat16)
    rows = jnp.concatenate([own, rest], axis=0).astype(jnp.float32)
    rows = jnp.roll(rows, own.shape[0] * lax.axis_index("tensor"), axis=0)
    rows = lax.psum_scatter(rows, "tensor", scatter_dimension=0, tiled=True)
    return shifted(rows.astype(jnp.bfloat16), "section", by)


def local(
    activations,
    upstream_grad,
    stash_blocks,
    guest_blocks,
    norm_gain,
    query_weight,
    keyval_weight,
    output_weight,
    evict_marks,
):
    sections = lax.axis_size("section")
    section_index = lax.axis_index("section")
    current = activations[0]
    upstream = upstream_grad[0]
    stash_rows = stash_blocks[0]
    guest_rows = guest_blocks[0]
    row_count, model_width = current.shape
    current_rest = others_rows(current)
    upstream_rest = others_rows(upstream)

    own_marks = lax.dynamic_index_in_dim(evict_marks, section_index, 0, keepdims=False)
    mirror_marks = lax.dynamic_index_in_dim(
        evict_marks, sections - 1 - section_index, 0, keepdims=False
    )
    pack_own, own_mask = packing(own_marks, row_count)
    pack_mirror, _ = packing(mirror_marks, row_count)
    guests_back = mirrored(nn(pack_mirror, guest_rows).astype(jnp.bfloat16))
    arrived = mirrored(nn(pack_own, current).astype(jnp.bfloat16))
    back_rows = jnp.where(own_mask, tn(pack_own, guests_back).astype(jnp.bfloat16), stash_rows)
    back_rest = others_rows(back_rows)
    held_rows = tn(pack_mirror, arrived).astype(jnp.bfloat16)
    kept_rows = jnp.where(own_mask, jnp.zeros_like(current), current)

    first = (lax.axis_index("tensor") * row_count).astype(jnp.int32)[None]
    keyval_cols = keyval_weight.shape[3]
    keyval_flat = keyval_weight[0].reshape(model_width, 2, keyval_cols // HEAD_DIM, HEAD_DIM)
    keyval_flat = keyval_flat.transpose(0, 2, 1, 3).reshape(model_width, 2 * keyval_cols)
    weights = (query_weight[0], keyval_flat, output_weight[0])

    ahead_own, ahead_rest = forward_layer(first, current, current_rest, norm_gain, weights)
    next_input = summed_and_moved(ahead_own, ahead_rest, 1)
    grad_own, grad_rest = backward_layer(
        first, back_rows, back_rest, upstream, upstream_rest, norm_gain, weights
    )
    prev_grad = summed_and_moved(grad_own, grad_rest, -1)
    return (next_input[None], prev_grad[None], kept_rows[None], held_rows[None])


def solution(mesh):
    rows = P("section", "tensor", None)
    placed = (
        rows,
        rows,
        rows,
        rows,
        P("section", None),
        P("section", None, "tensor"),
        P("section", None, None, "tensor"),
        P("section", "tensor", None),
        P(),
    )
    return jax.shard_map(
        local, mesh=mesh, in_specs=placed, out_specs=(rows, rows, rows, rows), check_vma=False
    )
```

time: 566 us -> 182 us (0.32)
  waiting for transfers between devices: 386 us -> 49.7 us
  matrix products: 104 us -> 6.22 us
  Pallas kernels: 0 us -> 83.3 us
  local copies, waits for them, and re-layouts: 31.1 us -> 15.9 us
  between operations: 14.5 us -> 0.79 us
  other arithmetic: 16.1 us -> 4.8 us
  starting transfers between devices: 11.4 us -> 19.1 us
    ppermute x4 -> x7, waiting for transfers between devices: 185 us -> 38.2 us  [the longest x3 16.4 us: swapped(): return lax.ppermute(x, 'tensor', [(0, 1), (1, 0)])]
    psum x1 -> x0, waiting for transfers between devices: 108 us -> none  [local(): lax.psum(rounded.astype(jnp.float32).astype(jnp.bfloat16), 'tensor')]
    dot_general x14 -> x4, matrix products: 99.5 us -> 6.22 us  [the longest x2 4.02 us: tn(): lax.dot_general(a, b, (((0,), (0,)), ((), ())), preferred_element_type=jn...]
    pallas_call x0 -> x2, Pallas kernels: none -> 83.3 us  [layer_call(): pl.pallas_call(kernel, grid=(groups,), in_specs=[pl.BlockSpec(memory_spac...]
    all_gather x1 -> x0, waiting for transfers between devices: 71.4 us -> none  [local(): fragment = lax.all_gather(stacked, 'tensor', axis=0, tiled=True)]
    unnamed x34 -> x10, local copies, waits for them, and re-layouts: 17 us -> 0.03 us
    ppermute x2, waiting for transfers between devices: 20.9 us -> 11.5 us  [shifted(): return lax.ppermute(x, axis, pairs)]
    ppermute x4 -> x7, starting transfers between devices: 5.6 us -> 13.4 us  [the longest x2 5.92 us: mirrored(): lax.ppermute(x, 'section', [(i, peers - 1 - i) for i in range(peers)])]
  transfers between devices with their start and end apart: 8 -> 9, of which waited for: 8 -> 4; matrix products, arithmetic and copies ran while one was open for 2% -> 12% of each run, Pallas kernels for 0% -> 46%
where the time goes in v1:
time: 182 us; the launch traced here: 180 us
  Pallas kernels  83.3 us (46%)
  waiting for transfers between devices  49.7 us (27%)
  starting transfers between devices  19.1 us (10%)
  local copies, waits for them, and re-layouts  15.9 us (9%)
  matrix products  6.22 us (3%)
  other arithmetic  4.8 us (3%)
    pallas_call x2, Pallas kernels, layer_call(): pl.pallas_call(kernel, grid=(groups,), in_specs=[pl.BlockSpec(memory_spac...  83.3 us
    ppermute x3, waiting for transfers between devices, swapped(): return lax.ppermute(x, 'tensor', [(0, 1), (1, 0)])  16.4 us
    reshape x1, local copies, waits for them, and re-layouts, local(): keyval_flat.transpose(0, 2, 1, 3).reshape(model_width, 2 * keyval_cols)  14.3 us
    ppermute x2, waiting for transfers between devices, crossed(): return lax.ppermute(x, ('section', 'tensor'), pairs)  12.2 us
    ppermute x2, waiting for transfers between devices, shifted(): return lax.ppermute(x, axis, pairs)  11.5 us
    ppermute x2, waiting for transfers between devices, mirrored(): lax.ppermute(x, 'section', [(i, peers - 1 - i) for i in range(peers)])  9.65 us
    ppermute x2, starting transfers between devices, mirrored(): lax.ppermute(x, 'section', [(i, peers - 1 - i) for i in range(peers)])  5.92 us
    ppermute x2, starting transfers between devices, shifted(): return lax.ppermute(x, axis, pairs)  5.64 us
  transfers between devices with their start and end apart: 9, of which 4 were waited for; matrix products, arithmetic and copies ran while one was open for 12% of the time, Pallas kernels for 46%

profile of v1, /device:TPU:1, one launch (start us, length us, event | category | flops | bytes accessed | tf_op | source)
XLA Modules:
  0.0 179.8 jit_solution(14089088837327684474)
XLA Ops:
  0.7 0.9 compare_bitcast_fusion.1
  1.5 0.8 fusion.9
  2.3 0.1 copy.18
  2.4 0.1 multiply_reduce_fusion
  2.6 0.1 mul.37
  2.8 0.1 eq.69
  2.9 1.1 convolution_convert_fusion.3
  4.0 5.6 %collective-permute-start.3 = (bf16[64,4096]{1,0:T(8,128)(2,1)}, bf16[64,4096]{1,0:T(8,128)(2,1)}, u32[]{:S(2)}, u32[]{:S(2)}) collective-permute-start(bf16[64,4096]{1,0:T(8,128)(2,1)} %convolution_convert_fusion.3), channel_id=1, source_target_pairs={{0,30},{2,28},{4,26},{6,24},{8,22},{10,20},{12,18},{14,16},{16,14}... | collective-permute-start | bytes 1572872 | tf_op jit(solution)/shard_map/ppermute | solution.py:37
  9.7 1.2 collective-permute-start.5
  11.0 0.1 multiply_reduce_fusion.1
  11.2 0.1 eq.63
  11.4 0.1 mul.34
  11.5 1.1 convolution_convert_fusion.2
  12.6 0.3 collective-permute-start.8
  12.9 0.2 collective-permute-start
  13.1 9.6 %collective-permute-done.3 = bf16[64,4096]{1,0:T(8,128)(2,1)} collective-permute-done((bf16[64,4096]{1,0:T(8,128)(2,1)}, bf16[64,4096]{1,0:T(8,128)(2,1)}, u32[]{:S(2)}, u32[]{:S(2)}) %collective-permute-start.3) | collective-permute-done | bytes 524320 | tf_op jit(solution)/shard_map/ppermute | solution.py:37
  22.8 1.5 fusion.own_ref
  24.3 1.2 collective-permute-start.4
  25.6 1.1 broadcast_select_fusion
  26.7 14.3 %reshape.132.wkv_ref = bf16[4096,1024]{1,0:T(8,128)(2,1)} reshape(bf16[4096,4,2,128]{3,2,1,0:T(2,128)(2,1)} %bitcast.37) | data formatting | bytes 16777216 | tf_op jit(solution)/shard_map/reshape | solution.py:341
  41.0 16.4 %collective-permute-done.rest_ref = bf16[128,4096]{1,0:T(8,128)(2,1)} collective-permute-done((bf16[128,4096]{1,0:T(8,128)(2,1)S(1)}, bf16[128,4096]{1,0:T(8,128)(2,1)}, u32[]{:S(2)}, u32[]{:S(2)}) %collective-permute-start) | collective-permute-done | bytes 1048608 | tf_op jit(solution)/shard_map/ppermute | solution.py:41
  57.3 33.8 %forward_layer.1 = (bf16[128,4096]{1,0:T(8,128)(2,1)}, bf16[128,4096]{1,0:T(8,128)(2,1)}) custom-call(s32[1]{0:T(128)} %bitcast.first_ref, bf16[128,4096]{1,0:T(8,128)(2,1)} %bitcast.35, bf16[128,4096]{1,0:T(8,128)(2,1)} %collective-permute-done.rest_ref, f32[1,4096]{1,0:T(1,128)} %gain_ref.3, bf16[4096,2048]{1,0:T(8,128)(2,1)} %bitcast.31, ...), custom_call_target="tpu_custom_call" | custom-call | flops 10737418240 | bytes 44040192 | tf_op jit(solution)/shard_map/forward_layer/pallas_call | solution.py:221
  91.1 3.0 %collective-permute-start.1 = (bf16[128,4096]{1,0:T(8,128)(2,1)}, bf16[128,4096]{1,0:T(8,128)(2,1)S(1)}, u32[]{:S(2)}, u32[]{:S(2)}) collective-permute-start(bf16[128,4096]{1,0:T(8,128)(2,1)} %get-tuple-element.8), channel_id=1, source_target_pairs={{0,2},{2,4},{4,6},{6,8},{8,10},{10,12},{12,14},{14,16},{16,18},{18... | collective-permute-start | bytes 3145736 | tf_op jit(solution)/shard_map/ppermute | solution.py:24
  94.1 2.9 %collective-permute-start.2 = (bf16[128,4096]{1,0:T(8,128)(2,1)}, bf16[128,4096]{1,0:T(8,128)(2,1)S(1)}, u32[]{:S(2)}, u32[]{:S(2)}) collective-permute-start(bf16[128,4096]{1,0:T(8,128)(2,1)} %get-tuple-element.9), channel_id=1, source_target_pairs={{0,3},{1,2},{2,5},{3,4},{4,7},{5,6},{6,9},{7,8},{8,11},{9,10},{10,... | collective-permute-start | bytes 3145736 | tf_op jit(solution)/shard_map/ppermute | solution.py:32
  97.0 49.5 %backward_layer.1 = (bf16[128,4096]{1,0:T(8,128)(2,1)}, bf16[128,4096]{1,0:T(8,128)(2,1)}) custom-call(s32[1]{0:T(128)} %bitcast.first_ref, bf16[128,4096]{1,0:T(8,128)(2,1)} %copy-done.4, bf16[128,4096]{1,0:T(8,128)(2,1)} %collective-permute-done.4.rest_ref, bf16[128,4096]{1,0:T(8,128)(2,1)} %bitcast.39, ...), custom_call_target="tpu_custom_call" | custom-call | flops 17179869184 | bytes 46137344 | tf_op jit(solution)/shard_map/backward_layer/pallas_call | solution.py:221
  146.5 2.6 %collective-permute-start.6 = (bf16[128,4096]{1,0:T(8,128)(2,1)}, bf16[128,4096]{1,0:T(8,128)(2,1)S(1)}, u32[]{:S(2)}, u32[]{:S(2)}) collective-permute-start(bf16[128,4096]{1,0:T(8,128)(2,1)} %get-tuple-element.10), channel_id=1, source_target_pairs={{2,0},{4,2},{6,4},{8,6},{10,8},{12,10},{14,12},{16,14},{18,16},{20... | collective-permute-start | bytes 3145736 | tf_op jit(solution)/shard_map/ppermute | solution.py:24
  149.2 1.9 %collective-permute-start.7 = (bf16[128,4096]{1,0:T(8,128)(2,1)}, bf16[128,4096]{1,0:T(8,128)(2,1)S(1)}, u32[]{:S(2)}, u32[]{:S(2)}) collective-permute-start(bf16[128,4096]{1,0:T(8,128)(2,1)} %get-tuple-element.11), channel_id=1, source_target_pairs={{2,1},{3,0},{4,3},{5,2},{6,5},{7,4},{8,7},{9,6},{10,9},{11,8},{12,... | collective-permute-start | bytes 3145736 | tf_op jit(solution)/shard_map/ppermute | solution.py:32
  151.1 2.5 %fusion.1 = bf16[1,128,4096]{2,1,0:T(8,128)(2,1)} fusion(bf16[64,4096]{1,0:T(8,128)(2,1)} %collective-permute-done.8, s32[128]{0:T(128)S(1)} %add_select_fusion), kind=kOutput, calls=%fused_computation.3 | convolution fusion | flops 67641344 | bytes 1573376 | tf_op jit(solution)/shard_map/dot_general | solution.py:53
  153.6 1.3 fusion.2
  154.9 11.5 %collective-permute-done.6 = bf16[128,4096]{1,0:T(8,128)(2,1)S(1)} collective-permute-done((bf16[128,4096]{1,0:T(8,128)(2,1)}, bf16[128,4096]{1,0:T(8,128)(2,1)S(1)}, u32[]{:S(2)}, u32[]{:S(2)}) %collective-permute-start.6) | collective-permute-done | bytes 1048608 | tf_op jit(solution)/shard_map/ppermute | solution.py:24
  166.4 12.2 %collective-permute-done.7 = bf16[128,4096]{1,0:T(8,128)(2,1)S(1)} collective-permute-done((bf16[128,4096]{1,0:T(8,128)(2,1)}, bf16[128,4096]{1,0:T(8,128)(2,1)S(1)}, u32[]{:S(2)}, u32[]{:S(2)}) %collective-permute-start.7) | collective-permute-done | bytes 1048608 | tf_op jit(solution)/shard_map/ppermute | solution.py:32
  178.6 1.2 fusion.3
  (24 shorter events, 0.5 us)
Async XLA Ops:
  0.6 2.3 %copy-start = (bf16[1,128,4096]{2,1,0:T(8,128)(2,1)S(1)}, bf16[1,128,4096]{2,1,0:T(8,128)(2,1)}, u32[]{:S(2)}) copy-start(bf16[1,128,4096]{2,1,0:T(8,128)(2,1)} %param.12) | copy-start | bytes 3145732
  0.6 10.8 %copy-start.2 = (bf16[1,128,4096]{2,1,0:T(8,128)(2,1)S(1)}, bf16[1,128,4096]{2,1,0:T(8,128)(2,1)}, u32[]{:S(2)}) copy-start(bf16[1,128,4096]{2,1,0:T(8,128)(2,1)} %param.9) | copy-start | bytes 3145732
  0.7 22.1 %copy-start.3 = (bf16[1,128,4096]{2,1,0:T(8,128)(2,1)S(1)}, bf16[1,128,4096]{2,1,0:T(8,128)(2,1)}, u32[]{:S(2)}) copy-start(bf16[1,128,4096]{2,1,0:T(8,128)(2,1)} %param.11) | copy-start | bytes 3145732
  4.0 18.7 %collective-permute-start.3 = (bf16[64,4096]{1,0:T(8,128)(2,1)}, bf16[64,4096]{1,0:T(8,128)(2,1)}, u32[]{:S(2)}, u32[]{:S(2)}) collective-permute-start(bf16[64,4096]{1,0:T(8,128)(2,1)} %convolution_convert_fusion.3), channel_id=1, source_target_pairs={{0,30},{2,28},{4,26},{6,24},{8,22},{10,20},{12,18},{14,16},{16,14}... | collective-permute-start | bytes 1572872 | tf_op jit(solution)/shard_map/ppermute | solution.py:37
  9.7 87.4 %collective-permute-start.5 = (bf16[128,4096]{1,0:T(8,128)(2,1)}, bf16[128,4096]{1,0:T(8,128)(2,1)}, u32[]{:S(2)}, u32[]{:S(2)}) collective-permute-start(bf16[128,4096]{1,0:T(8,128)(2,1)} %bitcast.38), channel_id=1, source_target_pairs={{0,1},{1,0},{2,3},{3,2},{4,5},{5,4},{6,7},{7,6},{8,9},{9,8},{10,11... | collective-permute-start | bytes 3145736 | tf_op jit(solution)/shard_map/ppermute | solution.py:41
  12.6 138.5 %collective-permute-start.8 = (bf16[64,4096]{1,0:T(8,128)(2,1)}, bf16[64,4096]{1,0:T(8,128)(2,1)}, u32[]{:S(2)}, u32[]{:S(2)}) collective-permute-start(bf16[64,4096]{1,0:T(8,128)(2,1)} %convolution_convert_fusion.2), channel_id=1, source_target_pairs={{0,30},{2,28},{4,26},{6,24},{8,22},{10,20},{12,18},{14,16},{16,14}... | collective-permute-start | bytes 1572872 | tf_op jit(solution)/shard_map/ppermute | solution.py:37
  12.9 44.4 %collective-permute-start = (bf16[128,4096]{1,0:T(8,128)(2,1)S(1)}, bf16[128,4096]{1,0:T(8,128)(2,1)}, u32[]{:S(2)}, u32[]{:S(2)}) collective-permute-start(bf16[128,4096]{1,0:T(8,128)(2,1)S(1)} %bitcast.36), channel_id=1, source_target_pairs={{0,1},{1,0},{2,3},{3,2},{4,5},{5,4},{6,7},{7,6},{8,9},{9,8},{10,11... | collective-permute-start | bytes 3145736 | tf_op jit(solution)/shard_map/ppermute | solution.py:41
  24.3 16.7 %copy-start.4 = (bf16[128,4096]{1,0:T(8,128)(2,1)}, bf16[128,4096]{1,0:T(8,128)(2,1)S(1)}, u32[]{:S(2)}) copy-start(bf16[128,4096]{1,0:T(8,128)(2,1)S(1)} %fusion.own_ref) | copy-start | bytes 3145732
  24.3 72.7 %collective-permute-start.4 = (bf16[128,4096]{1,0:T(8,128)(2,1)S(1)}, bf16[128,4096]{1,0:T(8,128)(2,1)}, u32[]{:S(2)}, u32[]{:S(2)}) collective-permute-start(bf16[128,4096]{1,0:T(8,128)(2,1)S(1)} %fusion.own_ref), channel_id=1, source_target_pairs={{0,1},{1,0},{2,3},{3,2},{4,5},{5,4},{6,7},{7,6},{8,9},{9,8},{10,11... | collective-permute-start | bytes 3145736 | tf_op jit(solution)/shard_map/ppermute | solution.py:41
  91.1 62.5 %collective-permute-start.1 = (bf16[128,4096]{1,0:T(8,128)(2,1)}, bf16[128,4096]{1,0:T(8,128)(2,1)S(1)}, u32[]{:S(2)}, u32[]{:S(2)}) collective-permute-start(bf16[128,4096]{1,0:T(8,128)(2,1)} %get-tuple-element.8), channel_id=1, source_target_pairs={{0,2},{2,4},{4,6},{6,8},{8,10},{10,12},{12,14},{14,16},{16,18},{18... | collective-permute-start | bytes 3145736 | tf_op jit(solution)/shard_map/ppermute | solution.py:24
  94.1 59.5 %collective-permute-start.2 = (bf16[128,4096]{1,0:T(8,128)(2,1)}, bf16[128,4096]{1,0:T(8,128)(2,1)S(1)}, u32[]{:S(2)}, u32[]{:S(2)}) collective-permute-start(bf16[128,4096]{1,0:T(8,128)(2,1)} %get-tuple-element.9), channel_id=1, source_target_pairs={{0,3},{1,2},{2,5},{3,4},{4,7},{5,6},{6,9},{7,8},{8,11},{9,10},{10,... | collective-permute-start | bytes 3145736 | tf_op jit(solution)/shard_map/ppermute | solution.py:32
  146.5 19.9 %collective-permute-start.6 = (bf16[128,4096]{1,0:T(8,128)(2,1)}, bf16[128,4096]{1,0:T(8,128)(2,1)S(1)}, u32[]{:S(2)}, u32[]{:S(2)}) collective-permute-start(bf16[128,4096]{1,0:T(8,128)(2,1)} %get-tuple-element.10), channel_id=1, source_target_pairs={{2,0},{4,2},{6,4},{8,6},{10,8},{12,10},{14,12},{16,14},{18,16},{20... | collective-permute-start | bytes 3145736 | tf_op jit(solution)/shard_map/ppermute | solution.py:24
  149.2 29.4 %collective-permute-start.7 = (bf16[128,4096]{1,0:T(8,128)(2,1)}, bf16[128,4096]{1,0:T(8,128)(2,1)S(1)}, u32[]{:S(2)}, u32[]{:S(2)}) collective-permute-start(bf16[128,4096]{1,0:T(8,128)(2,1)} %get-tuple-element.11), channel_id=1, source_target_pairs={{2,1},{3,0},{4,3},{5,2},{6,5},{7,4},{8,7},{9,6},{10,9},{11,8},{12,... | collective-permute-start | bytes 3145736 | tf_op jit(solution)/shard_map/ppermute | solution.py:32
  153.6 26.2 %copy-start.1 = (bf16[1,128,4096]{2,1,0:T(8,128)(2,1)S(1)}, bf16[1,128,4096]{2,1,0:T(8,128)(2,1)}, u32[]{:S(2)}) copy-start(bf16[1,128,4096]{2,1,0:T(8,128)(2,1)} %param.12) | copy-start | bytes 3145732
